TPU v7x, 512 devices: a whole 4x8x8 slice. The times are simulated.
512 devices in a mesh: lon: 64 (over z, y_lo, core), lat: 8 (over x, y_hi).
Axes of the slice: x: 4, y: 8 (y_hi: 2, y_lo: 4; y = y_hi * 4 + y_lo), z: 8, core: 2. Of those that a mesh axis runs over, the one named last changes fastest.
Arguments:
- fields: bfloat16 [2, 96, 384, 512], P(None, 'lat', 'lon'), may hold values from -6 to 6
- w_fine_qkv: bfloat16 [512, 1536], P('lon'), may hold values from -0.25 to 0.25
- w_fine_out: bfloat16 [512, 512], P('lon'), may hold values from -0.25 to 0.25
- w_merge: bfloat16 [2048, 1024], P('lon'), may hold values from -0.125 to 0.125
- w_coarse_qkv: bfloat16 [1024, 3072], P('lon'), may hold values from -0.1875 to 0.1875
- w_up: bfloat16 [1024, 512], P('lon'), may hold values from -0.1875 to 0.1875
- coarse_mask: int32 [2, 48, 192], P(None, 'lat', 'lon'), may hold values 0 or 1
- cotangent: bfloat16 [2, 96, 384, 512], P(None, 'lat', 'lon'), may hold values from -6 to 6
Outputs:
- output: bfloat16 [2, 96, 384, 512], P(None, 'lat', 'lon')
- grad_fields: bfloat16 [2, 96, 384, 512], P(None, 'lat', 'lon')
All inputs are finite; a program needn't handle non-finite values. No bound on the sum of `coarse_mask` on one device may be relied on, other than what follows from the above.
Results may differ from a plain program's by a relative error of at most 0.024.
Values may be sent and summed in bfloat16 or wider, within the bound.
A program may use at most 128 MiB of HBM per device.

v0:
```python
import jax
import jax.numpy as jnp
from jax import lax
from jax.sharding import PartitionSpec as P

HD = 32
WLEV = 2
WLAT = 6
SHLAT = 3
SHLON = 6


NORM_EPS = 1e-05
FAR_SCORE = -1000000000.0
MASK_PENALTY = 4.0


def passed_along(shard, axis, by):
    size = lax.axis_size(axis)
    return lax.ppermute(shard, axis, [(i, (i + by) % size) for i in range(size)])


def swapped(shard, axis, apart):
    return lax.ppermute(shard, axis, [(i, i ^ 1 << apart) for i in range(lax.axis_size(axis))])


def for_sending(shard):

    def short(part):
        return part.astype(jnp.bfloat16) if part.dtype == jnp.float32 else part

    return jax.tree.map(short, shard)


def norm_rows(values):
    wide = values.astype(jnp.float32)
    centre = jnp.mean(wide, axis=-1, keepdims=True)
    spread = jnp.mean(jnp.square(wide - centre), axis=-1, keepdims=True)
    return ((wide - centre) * lax.rsqrt(spread + NORM_EPS)).astype(jnp.bfloat16)


def project(values, weight):
    flat_rows = values.reshape(-1, values.shape[-1])
    product = jnp.dot(flat_rows, weight, preferred_element_type=jnp.float32)
    return product.astype(jnp.bfloat16).reshape(values.shape[:-1] + (weight.shape[1],))


def add_round(first, second):
    return (first.astype(jnp.float32) + second.astype(jnp.float32)).astype(jnp.bfloat16)


def attend(query, key_rows, value_rows, bias):
    score_scale = query.shape[-1] ** (-0.5)
    scores = (
        jnp.einsum("bqhd,bkhd->bhqk", query, key_rows, preferred_element_type=jnp.float32)
        * score_scale
    )
    scores = scores + bias[:, None]
    row_peak = jnp.max(scores, axis=-1, keepdims=True)
    expo = jnp.exp(scores - row_peak)
    softmax_w = (expo / jnp.sum(expo, axis=-1, keepdims=True)).astype(jnp.bfloat16)
    mixed = jnp.einsum("bhqk,bkhd->bqhd", softmax_w, value_rows, preferred_element_type=jnp.float32)
    return mixed.astype(jnp.bfloat16)


def to_windows(values, win_levels, win_rows, win_cols):
    levels, lat_rows, lon_cols = values.shape[:3]
    trailing = values.shape[3:]
    values = values.reshape(
        (
            levels // win_levels,
            win_levels,
            lat_rows // win_rows,
            win_rows,
            lon_cols // win_cols,
            win_cols,
        )
        + trailing
    )
    perm_axes = (0, 2, 4, 1, 3, 5) + tuple(range(6, 6 + len(trailing)))
    values = jnp.transpose(values, perm_axes)
    count = levels // win_levels * (lat_rows // win_rows) * (lon_cols // win_cols)
    return values.reshape((count, win_levels * win_rows * win_cols) + trailing)


def from_windows(windows, levels, lat_rows, lon_cols, win_levels, win_rows, win_cols):
    trailing = windows.shape[2:]
    windows = windows.reshape(
        (
            levels // win_levels,
            lat_rows // win_rows,
            lon_cols // win_cols,
            win_levels,
            win_rows,
            win_cols,
        )
        + trailing
    )
    perm_axes = (0, 3, 1, 4, 2, 5) + tuple(range(6, 6 + len(trailing)))
    return jnp.transpose(windows, perm_axes).reshape((levels, lat_rows, lon_cols) + trailing)


def window_mix(query_in, kv_in, bias):
    levels, lat_rows, lon_cols, channels = query_in.shape
    heads = channels // HD
    key_cols = kv_in.shape[2]
    query = to_windows(
        query_in.reshape(levels, lat_rows, lon_cols, heads, HD), WLEV, WLAT, lon_cols
    )
    kv_win = to_windows(
        kv_in.reshape(levels, lat_rows, key_cols, 2, heads, HD), WLEV, WLAT, key_cols
    )
    mixed = attend(query, kv_win[:, :, 0], kv_win[:, :, 1], bias)
    return from_windows(mixed, levels, lat_rows, lon_cols, WLEV, WLAT, lon_cols).reshape(
        levels, lat_rows, lon_cols, channels
    )


def merge_block(fine, w_merge):
    levels, lat_rows, lon_cols, channels = fine.shape
    grouped = fine.reshape(levels, lat_rows // 2, 2, lon_cols // 2, 2, channels)
    grouped = jnp.transpose(grouped, (0, 1, 3, 2, 4, 5)).reshape(
        levels, lat_rows // 2, lon_cols // 2, 4 * channels
    )
    return project(norm_rows(grouped), w_merge)


def tail_block(fine, deeper, w_up):
    upward = project(deeper, w_up)
    spread_up = jnp.repeat(jnp.repeat(upward, 2, axis=1), 2, axis=2)
    return add_round(fine, spread_up)


def roll_in(field):
    left_edge = field
    arrived = passed_along(left_edge, "lon", -1)
    field = jnp.concatenate([field[:, :, SHLON:], arrived], axis=2)
    top_rows = field[:, :SHLAT]
    arrived = passed_along(top_rows, "lat", -1)
    return jnp.concatenate([field[:, SHLAT:], arrived], axis=1)


def roll_out(field):
    bottom_rows = field[:, -SHLAT:]
    arrived = passed_along(bottom_rows, "lat", 1)
    field = jnp.concatenate([arrived, field[:, : field.shape[1] - SHLAT]], axis=1)
    arrived = passed_along(field, "lon", 1)
    return jnp.concatenate([arrived, field[:, :, : field.shape[2] - SHLON]], axis=2)


def order_pair(own_part, other_part, is_first):
    first_half = jnp.where(is_first, own_part, other_part)
    second_half = jnp.where(is_first, other_part, own_part)
    return jnp.concatenate([first_half, second_half], axis=2)


def split_pair(joined, is_first):
    half_cols = joined.shape[2] // 2
    first_half = joined[:, :, :half_cols]
    second_half = joined[:, :, half_cols:]
    return (
        jnp.where(is_first, first_half, second_half),
        jnp.where(is_first, second_half, first_half),
    )


def quad_gather(values, mask, is_even, is_low):
    near_values, near_mask = swapped((values, mask), "lon", 0)
    pair_values = order_pair(values, near_values, is_even)
    pair_mask = order_pair(mask, near_mask, is_even)
    far_values, far_mask = (
        swapped(pair_values, "lon", 1),
        swapped(for_sending(pair_mask), "lon", 1).astype(pair_mask.dtype),
    )
    return (order_pair(pair_values, far_values, is_low), order_pair(pair_mask, far_mask, is_low))


def quad_return(grad_quad, is_even, is_low):
    own_pair, far_pair = split_pair(grad_quad, is_low)
    pair_grad = own_pair + swapped(far_pair, "lon", 1)
    own_part, near_part = split_pair(pair_grad, is_even)
    return own_part + swapped(near_part, "lon", 0)


def body(fields, w_fine_qkv, w_fine_out, w_merge, w_coarse_qkv, w_up, coarse_mask, cotangent):
    coarse_width = w_coarse_qkv.shape[1] // 3
    local_query = w_coarse_qkv[:, :coarse_width]
    local_pair = w_coarse_qkv[:, coarse_width:]
    full_fq, full_fo, full_m, w_query, w_pair, full_up = (
        lax.all_gather(w_fine_qkv, "lon", axis=0, tiled=True),
        lax.all_gather(w_fine_out, "lon", axis=0, tiled=True),
        lax.all_gather(w_merge, "lon", axis=0, tiled=True),
        lax.all_gather(local_query, "lon", axis=0, tiled=True),
        lax.all_gather(local_pair, "lon", axis=0, tiled=True),
        lax.all_gather(w_up, "lon", axis=0, tiled=True),
    )
    levels, lat_rows, lon_cols, fine_width = fields.shape
    lat_index = lax.axis_index("lat") * lat_rows + jnp.arange(lat_rows)
    seam_rows = lat_index >= lat_rows * lax.axis_size("lat") - SHLAT
    lon_index = lax.axis_index("lon")
    is_even = lon_index % 2 == 0
    is_low = lon_index // 2 % 2 == 0
    query_region = jnp.broadcast_to(seam_rows[None, :, None], (levels, lat_rows, lon_cols)).astype(
        jnp.float32
    )
    key_region = jnp.broadcast_to(
        seam_rows[None, :, None], (levels, lat_rows, 2 * lon_cols)
    ).astype(jnp.float32)
    query_win = to_windows(query_region, WLEV, WLAT, lon_cols)
    key_win = to_windows(key_region, WLEV, WLAT, 2 * lon_cols)
    fine_bias = jnp.where(
        query_win[:, :, None] == key_win[:, None, :], jnp.float32(0.0), jnp.float32(FAR_SCORE)
    )

    def fine_front(rolled):
        qkv = project(norm_rows(rolled), full_fq)
        return (qkv[..., :fine_width], qkv[..., fine_width:])

    def fine_core(query_in, pair_kv):
        return project(window_mix(query_in, pair_kv, fine_bias), full_fo)

    def merge_apply(skip):
        return merge_block(skip, full_m)

    def tail_apply(skip, deeper):
        return tail_block(skip, deeper, full_up)

    rolled = roll_in(fields)
    (fine_query, own_kv), front_pull = jax.vjp(fine_front, rolled)
    other_kv = swapped(own_kv, "lon", 0)
    pair_kv = order_pair(own_kv, other_kv, is_even)
    mixed_rolled, core_pull = jax.vjp(fine_core, fine_query, pair_kv)
    skip = add_round(fields, roll_out(mixed_rolled))
    coarse, merge_pull = jax.vjp(merge_apply, skip)
    normed, norm_pull = jax.vjp(norm_rows, coarse)
    quad_normed, quad_mask = quad_gather(normed, coarse_mask, is_even, is_low)
    mask_win = to_windows(quad_mask.astype(jnp.float32), WLEV, WLAT, quad_mask.shape[2])
    quad_bias = (-MASK_PENALTY * (1.0 - mask_win))[:, None, :]

    def coarse_apply(residual_in, own_normed, all_normed):
        query_in = project(own_normed, w_query)
        kv_in = project(all_normed, w_pair)
        return add_round(residual_in, window_mix(query_in, kv_in, quad_bias))

    deeper, coarse_pull = jax.vjp(coarse_apply, coarse, normed, quad_normed)
    output, tail_pull = jax.vjp(tail_apply, skip, deeper)
    grad_skip_tail, grad_deeper = tail_pull(cotangent)
    grad_residual, grad_own, grad_all = coarse_pull(grad_deeper)
    grad_normed = grad_own + quad_return(grad_all, is_even, is_low)
    (grad_norm_in,) = norm_pull(grad_normed)
    grad_coarse = grad_residual + grad_norm_in
    (grad_skip_merge,) = merge_pull(grad_coarse)
    grad_skip = grad_skip_tail + grad_skip_merge
    grad_query, grad_pair = core_pull(roll_in(grad_skip))
    own_grad, other_grad = split_pair(grad_pair, is_even)
    grad_kv = own_grad + swapped(other_grad, "lon", 0)
    (grad_rolled,) = front_pull((grad_query, grad_kv))
    grad_fields = grad_skip + roll_out(grad_rolled)
    return (output, grad_fields)


def solution(mesh):
    placed = (
        P(None, "lat", "lon", None),
        P("lon", None),
        P("lon", None),
        P("lon", None),
        P("lon", None),
        P("lon", None),
        P(None, "lat", "lon"),
        P(None, "lat", "lon", None),
    )
    return jax.shard_map(
        body,
        mesh=mesh,
        in_specs=placed,
        out_specs=(P(None, "lat", "lon", None), P(None, "lat", "lon", None)),
        check_vma=False,
    )
```

profile of v0, /device:TPU:6, one launch (start us, length us, event | category | flops | bytes accessed | tf_op | source)
XLA Modules:
  0.0 753.3 jit_solution(13732080243345193123)
XLA Ops:
  12.4 13.4 %collective-permute-start = (bf16[2,12,6,512]{3,0,2,1:T(2,128)(2,1)}, bf16[2,12,6,512]{3,0,2,1:T(2,128)(2,1)S(1)}, u32[]{:S(2)}, u32[]{:S(2)}) collective-permute-start(bf16[2,12,6,512]{3,0,2,1:T(2,128)(2,1)} %param.8), channel_id=1, source_target_pairs={{0,504},{8,0},{16,8},{24,16},{32,24},{40,32},{48,40},{56,48},{64,5... | collective-permute-start | bytes 442376 | tf_op jit(solution)/shard_map/ppermute | solution.py:20
  28.5 77.3 %all_gather.19 = bf16[512,512]{1,0:T(8,128)(2,1)S(1)} all-gather(bf16[8,512]{1,0:T(8,128)(2,1)} %param.10), channel_id=1, replica_groups=mesh['lon'=64,'lat'=8] {'lon'}, dimensions={0}, use_global_device_ids=true | all-gather | bytes 532480 | tf_op jit(solution)/shard_map/all_gather | solution.py:191
  105.8 5.5 collective-permute-start.1
  111.8 3.8 collective-permute-done.1
  117.0 14.6 %all-gather.6.cloned.1.call-done = bf16[512,1536]{1,0:T(8,128)(2,1)} async-done(((bf16[8,1536]{1,0:T(8,128)(2,1)}), bf16[512,1536]{1,0:T(8,128)(2,1)}) %all-gather.6.cloned.1.call-update) | async-done | bytes 1572880 | tf_op jit(solution)/shard_map/all_gather | solution.py:190
  141.9 3.3 reshape.437
  152.8 2.7 convert_reduce_fusion
  161.9 7.3 collective-permute-start.3
  169.4 3.2 collective-permute-start.8
  174.0 2.4 collective-permute-start.4
  178.0 7.8 %collective-permute-done.4 = bf16[2,12,6,512]{3,2,1,0:T(8,128)(2,1)S(1)} collective-permute-done((bf16[2,12,6,512]{3,2,1,0:T(8,128)(2,1)}, bf16[2,12,6,512]{3,2,1,0:T(8,128)(2,1)S(1)}, u32[]{:S(2)}, u32[]{:S(2)}) %collective-permute-start.4) | collective-permute-done | bytes 147488 | tf_op jit(solution)/shard_map/ppermute | solution.py:20
  189.2 62.8 %all-gather.8.cloned.1.call-done = bf16[2048,1024]{1,0:T(8,128)(2,1)} async-done(((bf16[32,1024]{1,0:T(8,128)(2,1)}), bf16[2048,1024]{1,0:T(8,128)(2,1)}) %all-gather.8.cloned.1.call-update) | async-done | bytes 4194320 | tf_op jit(solution)/shard_map/all_gather | solution.py:192
  252.0 3.8 fusion.83
  266.3 103.2 %all-gather.14.cloned.1.call-done = bf16[1024,512]{1,0:T(8,128)(2,1)} async-done(((bf16[16,512]{1,0:T(8,128)(2,1)}), bf16[1024,512]{1,0:T(8,128)(2,1)}) %all-gather.14.cloned.1.call-update) | async-done | bytes 1048592 | tf_op jit(solution)/shard_map/all_gather | solution.py:195
  381.1 3.2 collective-permute-start.6
  384.3 103.2 %all-gather.12.cloned.1.call-done = bf16[1024,1024]{1,0:T(8,128)(2,1)} async-done(((bf16[16,1024]{1,0:T(8,128)(2,1)}), bf16[1024,1024]{1,0:T(8,128)(2,1)}) %all-gather.12.cloned.1.call-update) | async-done | bytes 2097168 | tf_op jit(solution)/shard_map/all_gather | solution.py:193
  487.6 2.7 convolution_convert_fusion.18
  496.0 111.8 %all-gather.10.cloned.1.call-done = bf16[1024,2048]{1,0:T(8,128)(2,1)} async-done(((bf16[16,2048]{1,0:T(8,128)(2,1)}), bf16[1024,2048]{1,0:T(8,128)(2,1)}) %all-gather.10.cloned.1.call-update) | async-done | bytes 4194320 | tf_op jit(solution)/shard_map/all_gather | solution.py:194
  607.8 3.9 convolution_convert_fusion
  626.8 3.4 collective-permute-start.9
  630.2 2.7 convolution_convert_fusion.9
  633.0 2.9 collective-permute-done.9
  642.4 2.6 fusion.50
  652.5 4.4 multiply_reduce_fusion
  667.4 5.0 collective-permute-start.11
  675.1 7.9 %collective-permute-start.12 = (bf16[2,3,6,512]{3,0,2,1:T(2,128)(2,1)S(1)}, bf16[2,3,6,512]{3,0,2,1:T(2,128)(2,1)S(1)}, u32[]{:S(2)}, u32[]{:S(2)}) collective-permute-start(bf16[2,3,6,512]{3,0,2,1:T(2,128)(2,1)S(1)} %slice.103), channel_id=1, source_target_pairs={{0,7},{1,0},{2,1},{3,2},{4,3},{5,4},{6,5},{7,6},{8,15},{9,8},{10,9... | collective-permute-start | bytes 110600 | tf_op jit(solution)/shard_map/ppermute | solution.py:20
  683.1 2.9 fusion.27
  706.2 4.1 reshape.480
  713.4 2.7 fusion.29
  723.8 6.8 collective-permute-start.14
  731.1 4.1 collective-permute-done.14
  738.4 7.4 collective-permute-done.15
  (353 shorter events, 144.8 us)
Async XLA Ops:
  7.2 124.5 %all-gather.6.cloned.1.call-start = ((), (), s32[]{:S(2)}) async-start(), calls=%async_computation | async-start | bytes 1597440 | tf_op jit(solution)/shard_map/all_gather | solution.py:190
  7.9 244.1 %all-gather.8.cloned.1.call-start = ((), (), s32[]{:S(2)}) async-start(), calls=%async_computation.1 | async-start | bytes 4259840 | tf_op jit(solution)/shard_map/all_gather | solution.py:192
  8.6 360.9 %all-gather.14.cloned.1.call-start = ((), (), s32[]{:S(2)}) async-start(), calls=%async_computation.4 | async-start | bytes 1064960 | tf_op jit(solution)/shard_map/all_gather | solution.py:195
  9.4 478.2 %all-gather.12.cloned.1.call-start = ((), (), s32[]{:S(2)}) async-start(), calls=%async_computation.3 | async-start | bytes 2129920 | tf_op jit(solution)/shard_map/all_gather | solution.py:193
  10.8 597.0 %all-gather.10.cloned.1.call-start = ((), (), s32[]{:S(2)}) async-start(), calls=%async_computation.2 | async-start | bytes 4259840 | tf_op jit(solution)/shard_map/all_gather | solution.py:194
  12.4 93.5 %collective-permute-start = (bf16[2,12,6,512]{3,0,2,1:T(2,128)(2,1)}, bf16[2,12,6,512]{3,0,2,1:T(2,128)(2,1)S(1)}, u32[]{:S(2)}, u32[]{:S(2)}) collective-permute-start(bf16[2,12,6,512]{3,0,2,1:T(2,128)(2,1)} %param.8), channel_id=1, source_target_pairs={{0,504},{8,0},{16,8},{24,16},{32,24},{40,32},{48,40},{56,48},{64,5... | collective-permute-start | bytes 442376 | tf_op jit(solution)/shard_map/ppermute | solution.py:20
  26.6 110.8 %collective-permute-start.7 = (s32[2,6,3]{2,1,0:T(8,128)S(1)}, s32[2,6,3]{2,1,0:T(8,128)S(1)}, u32[]{:S(2)}, u32[]{:S(2)}) collective-permute-start(s32[2,6,3]{2,1,0:T(8,128)S(1)} %copy.242), channel_id=1, source_target_pairs={{0,8},{8,0},{16,24},{24,16},{32,40},{40,32},{48,56},{56,48},{64,72... | collective-permute-start | bytes 440 | tf_op jit(solution)/shard_map/ppermute | solution.py:24
  105.8 9.8 %collective-permute-start.1 = (bf16[2,3,6,512]{3,0,2,1:T(2,128)(2,1)S(1)}, bf16[2,3,6,512]{3,0,2,1:T(2,128)(2,1)S(1)}, u32[]{:S(2)}, u32[]{:S(2)}) collective-permute-start(bf16[2,3,6,512]{3,0,2,1:T(2,128)(2,1)S(1)} %slice.89), channel_id=1, source_target_pairs={{0,7},{1,0},{2,1},{3,2},{4,3},{5,4},{6,5},{7,6},{8,15},{9,8},{10,9... | collective-permute-start | bytes 110600 | tf_op jit(solution)/shard_map/ppermute | solution.py:20
  115.9 15.8 %copy-start.14 = (bf16[2,12,6,512]{3,0,2,1:T(2,128)(2,1)}, bf16[2,12,6,512]{3,0,2,1:T(2,128)(2,1)S(1)}, u32[]{:S(2)}) copy-start(bf16[2,12,6,512]{3,0,2,1:T(2,128)(2,1)S(1)} %get-tuple-element.24) | copy-start | bytes 442372
  116.0 15.7 %copy-start.17 = (f32[144,512]{1,0:T(8,128)}, f32[144,512]{1,0:T(8,128)S(1)}, u32[]{:S(2)}) copy-start(f32[144,512]{1,0:T(8,128)S(1)} %reshape.469) | copy-start | bytes 884740
  116.0 15.6 %copy-start.24 = (f32[2,12,6]{0,2,1:T(8,128)}, f32[2,12,6]{0,2,1:T(8,128)S(1)}, u32[]{:S(2)}) copy-start(f32[2,12,6]{0,2,1:T(8,128)S(1)} %broadcast_multiply_fusion) | copy-start | bytes 1732
  133.7 5.4 collective-permute-start.2
  136.3 16.5 %copy-start.8 = (f32[2,72,144]{2,1,0:T(8,128)}, f32[2,72,144]{2,1,0:T(8,128)S(1)}, u32[]{:S(2)}) copy-start(f32[2,72,144]{2,1,0:T(8,128)S(1)} %compare_select_fusion) | copy-start | bytes 248836
  160.0 26.5 %copy-start.38 = (bf16[2,12,6,512]{3,0,2,1:T(2,128)(2,1)S(1)}, bf16[2,12,6,512]{3,0,2,1:T(2,128)(2,1)}, u32[]{:S(2)}) copy-start(bf16[2,12,6,512]{3,0,2,1:T(2,128)(2,1)} %param.8) | copy-start | bytes 442372
  161.9 11.3 %collective-permute-start.3 = (bf16[2,3,6,512]{3,2,1,0:T(8,128)(2,1)S(1)}, bf16[2,3,6,512]{3,2,1,0:T(8,128)(2,1)S(1)}, u32[]{:S(2)}, u32[]{:S(2)}) collective-permute-start(bf16[2,3,6,512]{3,2,1,0:T(8,128)(2,1)S(1)} %slice.94), channel_id=1, source_target_pairs={{0,1},{1,2},{2,3},{3,4},{4,5},{5,6},{6,7},{7,0},{8,9},{9,10},{10,1... | collective-permute-start | bytes 110600 | tf_op jit(solution)/shard_map/ppermute | solution.py:20
  169.4 7.1 collective-permute-start.8
  174.0 11.8 %collective-permute-start.4 = (bf16[2,12,6,512]{3,2,1,0:T(8,128)(2,1)}, bf16[2,12,6,512]{3,2,1,0:T(8,128)(2,1)S(1)}, u32[]{:S(2)}, u32[]{:S(2)}) collective-permute-start(bf16[2,12,6,512]{3,2,1,0:T(8,128)(2,1)} %pad_maximum_fusion.2), channel_id=1, source_target_pairs={{0,8},{8,16},{16,24},{24,32},{32,40},{40,48},{48,56},{56,64},{64,7... | collective-permute-start | bytes 442376 | tf_op jit(solution)/shard_map/ppermute | solution.py:20
  188.8 67.0 %copy-start.66 = (f32[36]{0:T(128)}, f32[36]{0:T(128)S(1)}, u32[]{:S(2)}) copy-start(f32[36]{0:T(128)S(1)} %rsqrt.45) | copy-start | bytes 436
  255.8 392.6 %copy-start.6 = (f32[36,1024]{1,0:T(8,128)}, f32[36,1024]{1,0:T(8,128)S(1)}, u32[]{:S(2)}) copy-start(f32[36,1024]{1,0:T(8,128)S(1)} %get-tuple-element.44) | copy-start | bytes 442372
  264.1 114.5 %collective-permute-start.5 = (bf16[2,6,3,1024]{3,2,1,0:T(4,128)(2,1)}, bf16[2,6,3,1024]{3,2,1,0:T(4,128)(2,1)}, u32[]{:S(2)}, u32[]{:S(2)}) collective-permute-start(bf16[2,6,3,1024]{3,2,1,0:T(4,128)(2,1)} %multiply_convert_fusion.2), channel_id=1, source_target_pairs={{0,8},{8,0},{16,24},{24,16},{32,40},{40,32},{48,56},{56,48},{64,72... | collective-permute-start | bytes 221192 | tf_op jit(solution)/shard_map/ppermute | solution.py:24
  381.1 110.9 %collective-permute-start.6 = (bf16[2,6,6,1024]{3,2,1,0:T(8,128)(2,1)}, bf16[2,6,6,1024]{3,2,1,0:T(8,128)(2,1)}, u32[]{:S(2)}, u32[]{:S(2)}) collective-permute-start(bf16[2,6,6,1024]{3,2,1,0:T(8,128)(2,1)} %pad_maximum_fusion.3), channel_id=1, source_target_pairs={{0,16},{8,24},{16,0},{24,8},{32,48},{40,56},{48,32},{56,40},{64,80... | collective-permute-start | bytes 442376 | tf_op jit(solution)/shard_map/ppermute | solution.py:24
  626.8 9.1 %collective-permute-start.9 = (bf16[2,6,6,1024]{3,2,1,0:T(8,128)(2,1)S(1)}, bf16[2,6,6,1024]{3,2,1,0:T(8,128)(2,1)S(1)}, u32[]{:S(2)}, u32[]{:S(2)}) collective-permute-start(bf16[2,6,6,1024]{3,2,1,0:T(8,128)(2,1)S(1)} %broadcast_select_fusion.3), channel_id=1, source_target_pairs={{0,16},{8,24},{16,0},{24,8},{32,48},{40,56},{48,32},{56,40},{64,80... | collective-permute-start | bytes 442376 | tf_op jit(solution)/shard_map/ppermute | solution.py:24
  637.4 5.1 collective-permute-start.10
  656.9 15.5 %copy-start.47 = (f32[2,16,72]{2,1,0:T(8,128)S(1)}, f32[2,16,72]{2,1,0:T(8,128)}, u32[]{:S(2)}) copy-start(f32[2,16,72]{2,1,0:T(8,128)} %copy-done.46) | copy-start | bytes 27652
  656.9 26.1 %copy-start.45 = (f32[32,36]{1,0:T(8,128)S(1)}, f32[32,36]{1,0:T(8,128)}, u32[]{:S(2)}) copy-start(f32[32,36]{1,0:T(8,128)} %copy-done.44) | copy-start | bytes 13828
  656.9 26.1 %copy-start.51 = (f32[32,36]{1,0:T(8,128)S(1)}, f32[32,36]{1,0:T(8,128)}, u32[]{:S(2)}) copy-start(f32[32,36]{1,0:T(8,128)} %copy-done.50) | copy-start | bytes 13828
  667.4 18.5 %copy-start.35 = (bf16[2,12,6,512]{3,0,2,1:T(2,128)(2,1)}, bf16[2,12,6,512]{3,0,2,1:T(2,128)(2,1)S(1)}, u32[]{:S(2)}) copy-start(bf16[2,12,6,512]{3,0,2,1:T(2,128)(2,1)S(1)} %add.142) | copy-start | bytes 442372
  667.4 7.6 %collective-permute-start.11 = (bf16[2,12,6,512]{3,0,2,1:T(2,128)(2,1)S(1)}, bf16[2,12,6,512]{3,0,2,1:T(2,128)(2,1)S(1)}, u32[]{:S(2)}, u32[]{:S(2)}) collective-permute-start(bf16[2,12,6,512]{3,0,2,1:T(2,128)(2,1)S(1)} %add.142), channel_id=1, source_target_pairs={{0,504},{8,0},{16,8},{24,16},{32,24},{40,32},{48,40},{56,48},{64,5... | collective-permute-start | bytes 442376 | tf_op jit(solution)/shard_map/ppermute | solution.py:20
  675.1 12.8 %collective-permute-start.12 = (bf16[2,3,6,512]{3,0,2,1:T(2,128)(2,1)S(1)}, bf16[2,3,6,512]{3,0,2,1:T(2,128)(2,1)S(1)}, u32[]{:S(2)}, u32[]{:S(2)}) collective-permute-start(bf16[2,3,6,512]{3,0,2,1:T(2,128)(2,1)S(1)} %slice.103), channel_id=1, source_target_pairs={{0,7},{1,0},{2,1},{3,2},{4,3},{5,4},{6,5},{7,6},{8,15},{9,8},{10,9... | collective-permute-start | bytes 110600 | tf_op jit(solution)/shard_map/ppermute | solution.py:20
  711.3 6.8 collective-permute-start.13
  723.8 11.4 %collective-permute-start.14 = (bf16[2,3,6,512]{3,0,2,1:T(2,128)(2,1)S(1)}, bf16[2,3,6,512]{3,0,2,1:T(2,128)(2,1)S(1)}, u32[]{:S(2)}, u32[]{:S(2)}) collective-permute-start(bf16[2,3,6,512]{3,0,2,1:T(2,128)(2,1)S(1)} %slice.106), channel_id=1, source_target_pairs={{0,1},{1,2},{2,3},{3,4},{4,5},{5,6},{6,7},{7,0},{8,9},{9,10},{10,1... | collective-permute-start | bytes 110600 | tf_op jit(solution)/shard_map/ppermute | solution.py:20
  735.4 10.4 %collective-permute-start.15 = (bf16[2,12,6,512]{3,0,2,1:T(2,128)(2,1)S(1)}, bf16[2,12,6,512]{3,0,2,1:T(2,128)(2,1)S(1)}, u32[]{:S(2)}, u32[]{:S(2)}) collective-permute-start(bf16[2,12,6,512]{3,0,2,1:T(2,128)(2,1)S(1)} %pad_maximum_fusion.6), channel_id=1, source_target_pairs={{0,8},{8,16},{16,24},{24,32},{32,40},{40,48},{48,56},{56,64},{64,7... | collective-permute-start | bytes 442376 | tf_op jit(solution)/shard_map/ppermute | solution.py:20
  (57 other events, 244.5 us)
Sparse Core Ops, SparseCore 0:
  10.1 121.4 all-gather.5
  133.8 118.2 all-gather.7
  254.2 115.2 all-gather.13
  371.5 116.0 all-gather.11
  489.6 118.1 all-gather.9
where the time goes:
time: 759 us; the launch traced here: 753 us
  waiting for transfers between devices  427 us (56%)
  local copies, waits for them, and re-layouts  82.3 us (11%)
  blocking collectives  77.3 us (10%)
  starting transfers between devices  71.1 us (9%)
  matrix products  45 us (6%)
  other arithmetic  35.6 us (5%)
  between operations  15.5 us (2%)
    all_gather x1, waiting for transfers between devices, body(): lax.all_gather(local_pair, 'lon', axis=0, tiled=True)  112 us
    all_gather x1, waiting for transfers between devices, body(): lax.all_gather(w_up, 'lon', axis=0, tiled=True)  103 us
    all_gather x1, waiting for transfers between devices, body(): lax.all_gather(local_query, 'lon', axis=0, tiled=True)  103 us
    all_gather x1, blocking collectives, body(): lax.all_gather(w_fine_out, 'lon', axis=0, tiled=True)  77.3 us
    all_gather x1, waiting for transfers between devices, body(): lax.all_gather(w_merge, 'lon', axis=0, tiled=True)  62.8 us
    ppermute x8, starting transfers between devices, passed_along(): lax.ppermute(shard, axis, [(i, (i + by) % size) for i in range(size)])  50.4 us
    ppermute x8, waiting for transfers between devices, passed_along(): lax.ppermute(shard, axis, [(i, (i + by) % size) for i in range(size)])  25.7 us
    dot_general x12, matrix products, project(): product = jnp.dot(flat_rows, weight, preferred_element_type=jnp.float32)  25.5 us
  transfers between devices with their start and end apart: 21, of which 12 were waited for; matrix products, arithmetic and copies ran while one was open for 11% of the time, Pallas kernels for 0%

commit v1 on v0

v1 whole, which is shorter than its diff:
```python
import functools
from types import SimpleNamespace

import jax
import jax.numpy as jnp
import ml_dtypes
import numpy as np
from jax import lax
from jax.experimental import pallas as pl
from jax.experimental.pallas import tpu as pltpu
from jax.sharding import PartitionSpec as P

HD = 32
SHLAT = 3
NORM_EPS = 1e-05
FAR_SCORE = -1000000000.0
MASK_PENALTY = 4.0

MESH = pl.DeviceIdType.MESH
OWN = 144
HALO = 48
HALO_REAL = 36
REAL_KEYS = 2 * OWN + 4 * HALO
KEYS = 512
DEPTH = 256
CROWS = 48
CREAL = 36
REAL_CKEYS = 4 * CROWS
CKEYS = 256
FINE = 512
COARSE = 1024
GROUP = 256
HEADS = 8
LEVELS, LAT_ROWS, LON_COLS = 2, 12, 6
LEVEL = LAT_ROWS * LON_COLS


def constants():
    token = np.arange(OWN)
    level, row, col = token // 72, token // 6 % 12, token % 6
    pick = np.zeros((4 * CROWS, OWN), np.float32)
    coarse_at = level * 18 + row // 2 * 3 + col // 2
    pick[(row % 2 * 2 + col % 2) * CROWS + coarse_at, token] = 1
    shrink = pick.reshape(4, CROWS, OWN).sum(0)
    edge = np.zeros((OWN, 4 * HALO), np.float32)
    for slot in range(4):
        low = 9 if slot < 2 else 0
        inside = (row >= low) & (row < low + 3)
        edge[token[inside], slot * HALO + (level * 18 + (row - low) * 6 + col)[inside]] = 1
    bands = np.zeros((8, KEYS), np.float32)
    bands[0] = -1
    own_band = np.where(row < 3, 0, np.where(row < 9, 1, 2))
    bands[0, :OWN] = own_band
    bands[0, OWN : 2 * OWN] = own_band
    for slot in range(4):
        start = 2 * OWN + slot * HALO
        bands[0, start : start + HALO_REAL] = 0 if slot < 2 else 2
        bands[1 + slot // 2, start : start + HALO] = 10
    own_bands = np.zeros((OWN, 128), np.float32) + own_band[:, None]
    rims = np.zeros((2 * HALO, OWN), np.float32)
    for start, low in ((0, 0), (HALO, 9)):
        inside = (row >= low) & (row < low + 3)
        rims[start + (level * 18 + (row - low) * 6 + col)[inside], token[inside]] = 1
    entry = np.arange(CREAL)
    mask_place = np.zeros((18, LEVELS, GROUP), np.float32)
    mask_place[entry % 18, entry // 18, entry] = 1

    def deep(a, depth=DEPTH):
        return np.pad(a, ((0, 0), (0, depth - a.shape[1])))

    return (
        deep(pick), deep(pick.T), deep(shrink), deep(shrink.T, 128), deep(edge),
        deep(rims), bands, own_bands, mask_place,
    )


def mm(a, b):
    return lax.dot_general(a, b, (((1,), (0,)), ((), ())), preferred_element_type=jnp.float32)


def mt(a, b):
    return lax.dot_general(a, b, (((1,), (1,)), ((), ())), preferred_element_type=jnp.float32)


def tm(a, b):
    return lax.dot_general(a, b, (((0,), (0,)), ((), ())), preferred_element_type=jnp.float32)


def short(a):
    return a.astype(jnp.bfloat16)


def wide(a):
    return a.astype(jnp.float32)


def deepened(a, depth=DEPTH):
    return jnp.concatenate([a, jnp.zeros((depth - a.shape[0], a.shape[1]), a.dtype)], axis=0)


def normed_rows(values):
    centre = jnp.mean(values, axis=-1, keepdims=True)
    off = values - centre
    inverse = lax.rsqrt(jnp.mean(off * off, axis=-1, keepdims=True) + NORM_EPS)
    return off * inverse, inverse


def norm_pull(values, grad):
    hat, inverse = normed_rows(values)
    along = jnp.mean(grad * hat, axis=-1, keepdims=True)
    return inverse * (grad - jnp.mean(grad, axis=-1, keepdims=True) - hat * along)


def head_lanes(head):
    return lax.broadcasted_iota(jnp.int32, (1, GROUP), 1) // HD == head


def stack_heads(target, block):
    rows = block.shape[0]
    for head in range(HEADS):
        target[pl.ds(head * rows, rows), :] = jnp.where(
            head_lanes(head), block, jnp.zeros_like(block)
        )


def join_heads(stacked, rows):
    total = jnp.where(head_lanes(0), stacked[:rows], 0.0)
    for head in range(1, HEADS):
        total = total + jnp.where(
            head_lanes(head), stacked[head * rows : (head + 1) * rows], 0.0
        )
    return short(total)


def blocks(count, step):
    def one(index, carry):
        step(index)
        return carry

    lax.fori_loop(0, count, one, 0)


def wide_columns(index, start=0, size=GROUP):
    return pl.ds(pl.multiple_of(start + index * size, size), size)


def lanes(group, start=0):
    if isinstance(group, int):
        return pl.ds(start + group * GROUP, GROUP)
    return pl.ds(pl.multiple_of(start + group * GROUP, GROUP), GROUP)


def attend(rows, channels, q, kv, bias, out, stack, scores, weights, pump):
    together = rows if rows >= OWN else HEADS * rows

    def one_group(group):
        stack_heads(stack, q[:, lanes(group)])
        scores[...] = mt(stack[...], kv[:, lanes(group)])
        if pump is not None:
            pump()

        def one_head(head, carry):
            spot = pl.ds(pl.multiple_of(head * together, 16), together)
            s = scores[spot, :] * (HD**-0.5) + bias[...]
            e = jnp.exp(s - jnp.max(s, axis=-1, keepdims=True))
            weights[group, spot, :] = short(e * (1.0 / jnp.sum(e, axis=-1, keepdims=True)))
            return carry

        lax.fori_loop(0, HEADS * rows // together, one_head, 0, unroll=4 if together == rows else 1)
        if pump is not None:
            pump()
        out[:, lanes(group)] = join_heads(mm(weights[group], kv[:, lanes(group, channels)]), rows)
        if pump is not None:
            pump()

    if pump is None:
        blocks(channels // GROUP, one_group)
    else:
        for group in range(channels // GROUP):
            one_group(group)


def attend_pull(rows, channels, q, kv, grad, dq, dkv, stack, scores, weights, inner):
    together = rows if rows >= OWN else HEADS * rows

    def one_group(group, carry):
        stack_heads(stack, grad[:, lanes(group)])
        scores[...] = mt(stack[...], kv[:, lanes(group, channels)])

        def one_head(head, carry):
            spot = pl.ds(pl.multiple_of(head * together, 16), together)
            p = wide(weights[group, spot, :])
            d = scores[spot, :]
            mean = jnp.sum(p * d, axis=-1, keepdims=True)
            inner[spot, :] = short(p * (d - mean) * (HD**-0.5))
            return carry

        lax.fori_loop(0, HEADS * rows // together, one_head, 0, unroll=4 if together == rows else 1)
        dkv[:, lanes(group, channels)] = short(tm(weights[group], stack[...]))
        dq[:, lanes(group)] = join_heads(mm(inner[...], kv[:, lanes(group)]), rows)
        stack_heads(stack, q[:, lanes(group)])
        dkv[:, lanes(group)] = short(tm(inner[...], stack[...]))
        return carry

    lax.fori_loop(0, channels // GROUP, one_group, 0)


def exchange_peers(size_lon, size_lat):
    lon, lat = lax.axis_index("lon"), lax.axis_index("lat")
    odd = lon % 2
    at = lambda lon_at, lat_at: {"lon": lon_at, "lat": lat_at}
    mate = (lon + 2 * odd - 1 + size_lon) % size_lon
    before, after = (lat + size_lat - 1) % size_lat, (lat + 1) % size_lat
    near = lon + 1 - 2 * odd
    step = 2 - 4 * (lon // 2 % 2)
    return SimpleNamespace(
        mate=at(mate, lat),
        before=at(lon, before),
        before_mate=at(mate, before),
        after=at(lon, after),
        after_mate=at(mate, after),
        quad=(at(near, lat), at(lon + step, lat), at(near + step, lat)),
        first=jnp.where(lat == 0, 1.0, 0.0),
        last=jnp.where(lat == size_lat - 1, 1.0, 0.0),
    )


def layer_scratch():
    bf = lambda *s: pltpu.VMEM(s, jnp.bfloat16)
    f32 = lambda *s: pltpu.VMEM(s, jnp.float32)
    return dict(
        xk=bf(KEYS, FINE), masks=f32(4, 8, GROUP),
        kn=bf(4, CROWS, COARSE), dn_send=bf(3, CROWS, COARSE), dn_got=bf(3, CROWS, COARSE),
        df_send=bf(KEYS, FINE), mate_got=bf(OWN, FINE), halo_got=bf(DEPTH, FINE),
        fq=bf(OWN, FINE), fkv=bf(KEYS, 2 * FINE), fbias=f32(OWN, KEYS), mixed=bf(OWN, FINE),
        fstack=bf(HEADS * OWN, GROUP), fscores=f32(HEADS * OWN, KEYS),
        fweights=bf(FINE // GROUP, HEADS * OWN, KEYS), finner=bf(HEADS * OWN, KEYS),
        dmix=bf(OWN, FINE), dfq=bf(OWN, FINE), dfkv=bf(KEYS, 2 * FINE),
        cq=bf(CROWS, COARSE), ckv=bf(CKEYS, 2 * COARSE), cbias=f32(1, CKEYS),
        cmixed=bf(CROWS, COARSE),
        cstack=bf(HEADS * CROWS, GROUP), cscores=f32(HEADS * CROWS, CKEYS),
        cweights=bf(COARSE // GROUP, HEADS * CROWS, CKEYS), cinner=bf(HEADS * CROWS, CKEYS),
        ddeep=bf(CROWS, COARSE), dcq=bf(CROWS, COARSE), dckv=bf(CKEYS, 2 * COARSE),
        skip=bf(OWN, FINE), coarse=bf(CROWS, COARSE), grad_skip=bf(OWN, FINE),
        grouped=bf(CROWS, 4 * FINE), mask_send=f32(4, 8, GROUP), x_in=bf(OWN + 2 * HALO, FINE),
        cot=bf(OWN, FINE),
        w_fq=bf(FINE, 3 * FINE), w_fo=bf(FINE, FINE), xn=bf(KEYS, FINE),
        group_normed=bf(CROWS, 4 * FINE), d_group=f32(CROWS, 4 * FINE),
        d_normed=f32(CROWS, COARSE), d_fine=f32(OWN, FINE), deeper=bf(CROWS, COARSE),
        d_up=bf(CROWS, FINE), d_coarse=bf(CROWS, COARSE), upward=bf(CROWS, FINE),
        fine_mixed=bf(OWN, FINE),
    )


COPIES = 224


def unpack(field, target):
    both = wide(field[...])
    for level in range(LEVELS):
        target[pl.ds(level * LEVEL, LEVEL), :] = short(both[:, level, :])


def pack(values, target):
    halves = [values[level * LEVEL : (level + 1) * LEVEL] for level in range(LEVELS)]
    target[...] = short(jnp.stack(halves, axis=1))


def layer(peers, send, steps, field, cot_field, mask_field, consts, out, grad_out, full, ready, s):
    pick, pick_t, shrink, spread, edge, rims, bands, own_bands, mask_place = consts

    def pump(count=1):
        for _ in range(count):
            next(steps, None)

    def need(name):
        while name not in ready:
            next(steps, None)

    def columns_of(name, index, start=0):
        if name == FQ:
            return s.w_fq[:, wide_columns(index, start)]
        if name == FO:
            return s.w_fo[:, wide_columns(index, start)]
        return full[name][:, :, :, :, wide_columns(index, start)].reshape(-1, GROUP)

    def rows_of(name, index, columns=slice(None)):
        if name in (FQ, FO):
            rows = pl.ds(pl.multiple_of(index * GROUP, GROUP), GROUP)
            return (s.w_fq if name == FQ else s.w_fo)[rows, columns]
        slabs = GROUP // (2 * NY * full[name].shape[3])
        part = full[name][pl.ds(index * slabs, slabs), :, :, :, columns]
        return part.reshape(GROUP, part.shape[-1])

    def project(target, source, name, start=0):
        need(name)

        def step(index):
            target[:, wide_columns(index)] = short(mm(source[...], columns_of(name, index, start)))

        blocks(target.shape[-1] // GROUP, step)

    x_in, cot = s.x_in, s.cot
    unpack(field, x_in)
    rim_rows = mm(short(rims[...]), deepened(x_in[pl.ds(0, OWN), :]))
    x_in[pl.ds(OWN, 2 * HALO), :] = short(rim_rows)
    mask_row = jnp.zeros((1, GROUP), jnp.float32)
    for col in range(3):
        entries = -MASK_PENALTY * (1.0 - mask_field[col].astype(jnp.float32))
        for row in range(6):
            placed = entries[:, row : row + 1] * mask_place[row * 3 + col]
            mask_row = mask_row + jnp.sum(placed, axis=0, keepdims=True)
    lane = lax.broadcasted_iota(jnp.int32, (1, GROUP), 1)
    absent = (lane >= CREAL) & (lane < CROWS)
    mask_row = jnp.broadcast_to(jnp.where(absent, FAR_SCORE, mask_row), (8, GROUP))
    mask_in, masks = s.mask_send, s.masks
    mask_in[0] = mask_row
    for j in range(1, 4):
        mask_in[j] = pltpu.roll(mask_row, j * CROWS, 1)

    xk = s.xk
    top, bottom = x_in.at[pl.ds(OWN, HALO)], x_in.at[pl.ds(OWN + HALO, HALO)]
    slot = lambda ref, i: ref.at[pl.ds(2 * OWN + i * HALO, HALO)]
    opening = [
        send(x_in.at[pl.ds(0, OWN)], xk.at[pl.ds(OWN, OWN)], peers.mate),
        send(bottom, slot(xk, 0), peers.after),
        send(bottom, slot(xk, 1), peers.after_mate),
        send(top, slot(xk, 2), peers.before),
        send(top, slot(xk, 3), peers.before_mate),
    ]
    mask_copies = [
        send(mask_in.at[j + 1], masks.at[j + 1], peers.quad[j]) for j in range(3)
    ]
    pump(2)
    xk[pl.ds(0, OWN), :] = x_in[pl.ds(0, OWN), :]
    xk[pl.ds(REAL_KEYS, KEYS - REAL_KEYS), :] = jnp.zeros((KEYS - REAL_KEYS, FINE), jnp.bfloat16)
    halo_got = s.halo_got
    halo_got[pl.ds(4 * HALO, DEPTH - 4 * HALO), :] = jnp.zeros((DEPTH - 4 * HALO, FINE), jnp.bfloat16)
    masks[0] = mask_in[0]
    key_bands = bands[0:1] + peers.first * bands[1:2] + peers.last * bands[2:3]
    s.fbias[...] = jnp.where(own_bands[:, 0:1] == key_bands, 0.0, FAR_SCORE)
    pump(2)
    unpack(cot_field, cot)
    pump(2)
    for copy in opening:
        copy.wait_recv()

    def norm_step(index):
        rows = pl.ds(pl.multiple_of(index * 128, 128), 128)
        s.xn[rows, :] = short(normed_rows(wide(xk[rows, :]))[0])

    blocks(KEYS // 128, norm_step)
    pump(2)
    project(s.fq, s.xn.at[pl.ds(0, OWN)], FQ)
    pump()
    project(s.fkv, s.xn, FQ, FINE)
    pump()
    attend(OWN, FINE, s.fq, s.fkv, s.fbias, s.mixed, s.fstack, s.fscores, s.fweights, pump)
    project(s.fine_mixed, s.mixed, FO)
    pump()
    skip = short(wide(x_in[pl.ds(0, OWN), :]) + wide(s.fine_mixed[...]))
    s.skip[...] = skip

    picked = short(mm(short(pick[...]), deepened(skip)))
    for part in range(4):
        s.grouped[:, pl.ds(part * FINE, FINE)] = picked[part * CROWS : (part + 1) * CROWS]
    s.group_normed[...] = short(normed_rows(wide(s.grouped[...]))[0])
    pump()
    project(s.coarse, s.group_normed, MG)
    kn = s.kn
    kn[0] = short(normed_rows(wide(s.coarse[...]))[0])
    quad_copies = [send(kn.at[0], kn.at[j + 1], peers.quad[j]) for j in range(3)]

    cot_here = cot[...]
    s.d_up[...] = short(mm(short(shrink[...]), deepened(cot_here)))
    need(UP)

    def up_step(index):
        s.ddeep[:, wide_columns(index)] = short(mt(s.d_up[...], rows_of(UP, index)))

    blocks(COARSE // GROUP, up_step)
    project(s.cq, kn.at[0], CQ)
    for copy in mask_copies + quad_copies:
        copy.wait_recv()
    total_mask = masks[0] + masks[1] + masks[2] + masks[3]
    s.cbias[...] = jnp.where(lane >= REAL_CKEYS, FAR_SCORE, total_mask[:1, :CKEYS])

    def ckv_step(index):
        s.ckv[pl.ds(0, REAL_CKEYS), wide_columns(index)] = short(
            mm(kn[...].reshape(REAL_CKEYS, COARSE), columns_of(CQ, index, COARSE))
        )

    blocks(2 * COARSE // GROUP, ckv_step)
    s.ckv[pl.ds(REAL_CKEYS, CKEYS - REAL_CKEYS), :] = jnp.zeros(
        (CKEYS - REAL_CKEYS, 2 * COARSE), jnp.bfloat16
    )
    attend(CROWS, COARSE, s.cq, s.ckv, s.cbias, s.cmixed, s.cstack, s.cscores, s.cweights, None)
    s.deeper[...] = short(wide(s.coarse[...]) + wide(s.cmixed[...]))
    project(s.upward, s.deeper, UP)
    output = (wide(s.skip[...]) + mm(short(spread[...]), deepened(s.upward[...], 128)))
    pack(output, out)

    attend_pull(CROWS, COARSE, s.cq, s.ckv, s.ddeep, s.dcq, s.dckv, s.cstack, s.cscores, s.cweights, s.cinner)
    def all_step(index):
        at = wide_columns(index)
        d_all = mt(s.dckv[pl.ds(0, REAL_CKEYS), :], rows_of(CQ, index, pl.ds(COARSE, 2 * COARSE)))
        s.d_normed[:, at] = d_all[:CROWS]
        for j in range(3):
            s.dn_send[j, :, at] = short(d_all[(j + 1) * CROWS : (j + 2) * CROWS])

    blocks(COARSE // GROUP, all_step)
    back_copies = [
        send(s.dn_send.at[j], s.dn_got.at[j], peers.quad[j]) for j in range(3)
    ]

    def own_step(index):
        at = wide_columns(index)
        own_part = mt(s.dcq[...], rows_of(CQ, index, pl.ds(0, COARSE)))
        s.d_normed[:, at] = s.d_normed[:, at] + own_part

    blocks(COARSE // GROUP, own_step)
    for copy in back_copies:
        copy.wait_recv()
    d_normed = s.d_normed[...]
    for j in range(3):
        d_normed = d_normed + wide(s.dn_got[j])
    s.d_coarse[...] = short(wide(s.ddeep[...]) + norm_pull(wide(s.coarse[...]), d_normed))

    def merge_step(index):
        s.d_group[:, wide_columns(index)] = mt(s.d_coarse[...], rows_of(MG, index))

    blocks(4 * FINE // GROUP, merge_step)
    d_group = short(norm_pull(wide(s.grouped[...]), s.d_group[...]))
    d_picked = jnp.concatenate(
        [d_group[:, part * FINE : (part + 1) * FINE] for part in range(4)], axis=0
    )
    s.grad_skip[...] = short(wide(cot_here) + mm(short(pick_t[...]), deepened(d_picked)))

    def out_step(index):
        s.dmix[:, wide_columns(index)] = short(mt(s.grad_skip[...], rows_of(FO, index)))

    blocks(FINE // GROUP, out_step)
    attend_pull(OWN, FINE, s.fq, s.fkv, s.dmix, s.dfq, s.dfkv, s.fstack, s.fscores, s.fweights, s.finner)
    df_send = s.df_send

    def fine_step(index):
        at = wide_columns(index)
        df_all = mt(s.dfkv[...], rows_of(FQ, index, pl.ds(FINE, 2 * FINE)))
        s.d_fine[:, at] = df_all[:OWN]
        df_send[:, at] = short(df_all)

    blocks(FINE // GROUP, fine_step)
    halo_got = s.halo_got
    got = lambda i: halo_got.at[pl.ds(i * HALO, HALO)]
    end_copies = [
        send(df_send.at[pl.ds(OWN, OWN)], s.mate_got, peers.mate),
        send(slot(df_send, 0), got(0), peers.before),
        send(slot(df_send, 1), got(1), peers.before_mate),
        send(slot(df_send, 2), got(2), peers.after),
        send(slot(df_send, 3), got(3), peers.after_mate),
    ]

    def query_step(index):
        at = wide_columns(index)
        own_part = mt(s.dfq[...], rows_of(FQ, index, pl.ds(0, FINE)))
        s.d_fine[:, at] = s.d_fine[:, at] + own_part

    blocks(FINE // GROUP, query_step)
    for copy in end_copies:
        copy.wait_recv()
    d_fine = s.d_fine[...] + wide(s.mate_got[...])
    from_halo = s.fscores.at[pl.ds(0, OWN), :]
    from_halo[...] = mm(short(edge[...]), halo_got[...])
    d_fine = d_fine + from_halo[...]
    pulled = norm_pull(wide(x_in[pl.ds(0, OWN), :]), d_fine)
    pack(wide(s.grad_skip[...]) + pulled, grad_out)


NZ = 8
NY = 4
FQ, FO, MG, UP, CQ = range(5)
WEIGHTS = (FQ, FO, MG, UP, CQ)


def ring_peers():
    lon, lat = lax.axis_index("lon"), lax.axis_index("lat")
    z, y, c = lon // (2 * NY), lon // 2 % NY, lon % 2
    x, y_hi = lat // 2, lat % 2

    def at(dz, dy, core):
        row = y + dy + NY
        carried = (y_hi + row // NY + 1) % 2
        return {
            "lon": ((z + dz + NZ) % NZ * NY + row % NY) * 2 + core,
            "lat": x * 2 + carried,
        }

    peers = at(1, 0, c), at(-1, 0, c), at(0, 1, c), at(0, -1, c), at(0, 0, 1 - c)
    turn = jnp.where(x == 3, 1, -x)
    back = jnp.where(x == 3, -1, x)
    shift_core = jnp.where(x == 0, 1 - c, c)
    shift_to, shift_from = at(0, turn, shift_core), at(0, back, shift_core)
    along = [{"lon": lon, "lat": (x + d) % 4 * 2 + y_hi} for d in (1, 3)]
    rim = tuple(at(d, 0, c) for d in (2, -2, 3, -3, 4))
    return (x, y, z, c), peers + (*along, shift_to, shift_from) + rim


def gather_steps(spot, peers, own, full, send, local_sems, ready, s):
    x, y, z, c = spot
    up_z, down_z, up_y, down_y, twin, up_x, down_x, shift_to, _ = peers[:9]
    w = (x + y) % NY
    z_at = lambda dz: (z + dz + NZ) % NZ
    y_at = lambda dy: (y + dy + NY) % NY
    w_at = lambda dw: (w + dw + NY) % NY
    every = slice(None)
    here = lambda k: full[k].at[z, y, c]

    def arrived(copies):
        for copy in copies:
            copy.wait_recv()

    def pass_on(k, where, peer):
        view = full[k].at[where]
        return send(view, view, peer)

    def half(k, place, which):
        width = full[k].shape[-1] // 2
        return place + (every, pl.ds(which * width, width))

    twins = {name: [] for name in WEIGHTS}

    def to_twin(k, where):
        twins[k].append(pass_on(k, where, twin))

    locals_ = {}
    for index, k in enumerate(WEIGHTS):
        locals_[k] = pltpu.make_async_copy(own[k], here(k), local_sems.at[index])
        if k != CQ:
            locals_[k].start()

    near, far, wheel, ring, across = {}, {}, {}, {}, {}

    def yz_start(k):
        near[k] = [send(own[k], here(k), peer) for peer in (up_y, down_y)]

    def yz_far(k):
        arrived(near[k][:1])
        first = pass_on(k, half(k, (z, y_at(-1), c), 0), up_y)
        arrived(near[k][1:])
        far[k] = [first, pass_on(k, half(k, (z, y_at(1), c), 1), down_y)]

    def yz_round(k):
        arrived(far[k])
        locals_[k].wait()
        wheel[k] = [pass_on(k, (z, every, c), peer) for peer in (up_z, down_z)]
        to_twin(k, (z, every, c))

    def yz_step(k, step):
        arrived(wheel[k])
        if step < 3:
            wheel[k] = [
                pass_on(k, (z_at(-step), every, c), up_z),
                pass_on(k, (z_at(step), every, c), down_z),
            ]
        elif step == 3:
            wheel[k] = [
                pass_on(k, (z_at(-3), pl.ds(0, 2), c), up_z),
                pass_on(k, (z_at(3), pl.ds(2, 2), c), down_z),
            ]
        for d in (-step, step)[: 2 if step < 4 else 1]:
            to_twin(k, (z_at(d), every, c))

    def zy_start(k):
        ring[k] = [send(own[k], here(k), peer) for peer in (up_z, down_z)]

    def zy_step(k, step):
        arrived(ring[k])
        if step < 3:
            ring[k] = [
                pass_on(k, (z_at(-step), y, c), up_z),
                pass_on(k, (z_at(step), y, c), down_z),
            ]
        elif step == 3:
            ring[k] = [
                pass_on(k, half(k, (z_at(-3), y, c), 0), up_z),
                pass_on(k, half(k, (z_at(3), y, c), 1), down_z),
            ]

    def across_y(k, where):
        return [pass_on(k, (where, y, c), peer) for peer in (up_y, down_y)]

    def side(k):
        return (w_at, up_x, down_x) if k == CQ else (y_at, up_y, down_y)

    def chain_across(k, d):
        place, up, down = side(k)
        across[k, d % NZ] = [pass_on(k, (z_at(d), place(0), c), peer) for peer in (up, down)]

    def chain_step(k, step):
        place, _, _ = side(k)
        arrived(ring[k])
        if step < 3:
            ring[k] = [
                pass_on(k, (z_at(-step), place(0), c), up_z),
                pass_on(k, (z_at(step), place(0), c), down_z),
            ]
        elif step == 3:
            ring[k] = [
                pass_on(k, half(k, (z_at(-3), place(0), c), 0), up_z),
                pass_on(k, half(k, (z_at(3), place(0), c), 1), down_z),
            ]
        for d in (-step, step)[: 2 if step < 4 else 1]:
            chain_across(k, d)

    def chain_spread(k, dz, turn):
        place, up, down = side(k)
        arrived(across[k, dz])
        if turn == 0:
            last[k].append(pass_on(k, (z_at(dz), place(-1), c), up))
        else:
            last[k].append(pass_on(k, (z_at(dz), place(1), c), down))

    def chain_twins(k, offsets):
        place, _, _ = side(k)
        for d in offsets:
            to_twin(k, (every, place(d), c))

    last = {CQ: [], MG: []}
    shift = send(own[CQ], here(CQ), shift_to, wait_start=True)

    @pl.when(x == 0)
    def _():
        locals_[CQ].start()

    @pl.when(x > 0)
    def _():
        shift.start()

    fine = (FQ, FO)
    fine_z = [send(own[k], here(k), peer) for peer in (up_z, down_z) + peers[9:] for k in fine]
    ring[MG] = [send(own[MG], here(MG), peer) for peer in (up_z, down_z)]

    @pl.when(x == 0)
    def _():
        locals_[CQ].wait()

    @pl.when(x > 0)
    def _():
        shift.wait_recv()

    ring[CQ] = [pass_on(CQ, (z, w, c), peer) for peer in (up_z, down_z)]
    chain_across(CQ, 0)
    yield
    arrived(fine_z)
    fine_y = []
    for k in fine:
        locals_[k].wait()
        fine_y += across_y(k, every)
    for k in fine:
        to_twin(k, (every, y, c))
    across[MG, 0] = [send(own[MG], here(MG), peer) for peer in (up_y, down_y)]
    yz_start(UP)
    yield
    chain_step(CQ, 1)
    chain_step(MG, 1)
    yield
    chain_step(CQ, 2)
    chain_step(MG, 2)
    yield
    arrived(fine_y)
    fine_far = []
    for k in fine:
        fine_far += [
            pass_on(k, (pl.ds(0, 4), y_at(-1), c), up_y),
            pass_on(k, (pl.ds(4, 4), y_at(1), c), down_y),
        ]
    for k in fine:
        to_twin(k, (every, y_at(-1), c))
        to_twin(k, (every, y_at(1), c))
    chain_step(CQ, 3)
    chain_step(MG, 3)
    yz_far(UP)
    yield
    arrived(fine_far)
    for k in fine:
        to_twin(k, (every, y_at(2), c))
    chain_step(CQ, 4)
    chain_step(MG, 4)
    locals_[MG].wait()
    yield
    chain_spread(CQ, 0, 0)
    chain_spread(MG, 0, 0)
    chain_twins(CQ, (0,))
    chain_twins(MG, (0,))
    yz_round(UP)
    yield
    arrived(twins[FQ])

    def tidy(part):
        columns = wide_columns(part, 0, FINE)
        s.w_fq[:, columns] = short(wide(full[FQ][:, :, :, :, columns]).reshape(FINE, FINE))

    blocks(3, tidy)
    ready.add(FQ)
    chain_spread(CQ, 7, 1)
    chain_spread(MG, 7, 1)
    yield
    arrived(twins[FO])
    s.w_fo[...] = short(wide(full[FO][...]).reshape(FINE, FINE))
    ready.add(FO)
    chain_spread(CQ, 1, 0)
    chain_spread(MG, 1, 0)
    yield
    chain_spread(CQ, 6, 1)
    chain_spread(MG, 6, 1)
    yz_step(UP, 1)
    yield
    chain_spread(CQ, 2, 0)
    chain_spread(MG, 2, 0)
    yield
    chain_spread(CQ, 5, 1)
    chain_spread(MG, 5, 1)
    yz_step(UP, 2)
    yield
    chain_spread(CQ, 3, 0)
    chain_spread(MG, 3, 0)
    yield
    chain_spread(CQ, 4, 1)
    chain_spread(MG, 4, 1)
    chain_twins(MG, (-1, 1))
    chain_twins(CQ, (-1, 1))
    yz_step(UP, 3)
    yield
    arrived(last[MG])
    chain_twins(MG, (2,))
    yield
    arrived(last[CQ])
    chain_twins(CQ, (2,))
    yz_step(UP, 4)
    yield
    arrived(twins[MG])
    ready.add(MG)
    yield
    arrived(twins[CQ])
    ready.add(CQ)
    yield
    arrived(twins[UP])
    ready.add(UP)

    @pl.when(x > 0)
    def _():
        shift.wait_send()


def layer_kernel(size_lon, size_lat, names, *refs):
    field, cot_field, mask_field = refs[:3]
    consts, held = refs[3:12], refs[12:17]
    out, grad_out = refs[17:19]
    scratch = SimpleNamespace(**dict(zip(names, refs[19 : 19 + len(names)])))
    rest = refs[19 + len(names) :]
    full = dict(zip(WEIGHTS, rest[: len(WEIGHTS)]))
    send_sems, recv_sems, local_sems = rest[len(WEIGHTS) :]
    own = dict(zip(WEIGHTS, held))
    peers = exchange_peers(size_lon, size_lat)
    spot, rings = ring_peers()
    barrier = pltpu.get_barrier_semaphore()
    everyone = [peers.mate, peers.before, peers.before_mate, peers.after, peers.after_mate]
    everyone += list(peers.quad) + list(rings)
    for peer in everyone:
        pl.semaphore_signal(barrier, inc=1, device_id=peer, device_id_type=MESH)
    pl.semaphore_wait(barrier, len(everyone))
    started = []

    def send(source, target, peer, wait_start=False):
        index = len(started)
        assert index < COPIES
        copy = pltpu.make_async_remote_copy(
            src_ref=source, dst_ref=target, send_sem=send_sems.at[index],
            recv_sem=recv_sems.at[index], device_id=peer, device_id_type=MESH,
        )
        if not wait_start:
            copy.start()
        started.append(None if wait_start else copy)
        return copy

    ready = set()
    steps = gather_steps(spot, rings, own, full, send, local_sems, ready, scratch)
    layer(
        peers, send, steps, field, cot_field, mask_field, consts, out, grad_out, full, ready, scratch
    )
    for copy in started:
        if copy is not None:
            copy.wait_send()


def run_layer(mesh, fields, cotangent, coarse_mask, held):
    scratch = layer_scratch()
    vmem = pl.BlockSpec(memory_space=pltpu.VMEM)
    rows = (LEVEL, LEVELS, FINE)
    flat = lambda part: part.transpose(1, 2, 0, 3).reshape(rows)
    consts = constants()
    out, grad = pl.pallas_call(
        functools.partial(layer_kernel, mesh.shape["lon"], mesh.shape["lat"], tuple(scratch)),
        out_shape=[jax.ShapeDtypeStruct(rows, jnp.bfloat16)] * 2,
        in_specs=[vmem] * (3 + len(consts)) + [pl.BlockSpec(memory_space=pl.ANY)] * 5,
        out_specs=[vmem] * 2,
        scratch_shapes=list(scratch.values())
        + [pltpu.VMEM((NZ, NY, 2) + held[name].shape, jnp.bfloat16) for name in WEIGHTS]
        + [
            pltpu.SemaphoreType.DMA((COPIES,)),
            pltpu.SemaphoreType.DMA((COPIES,)),
            pltpu.SemaphoreType.DMA((len(WEIGHTS),)),
        ],
        compiler_params=pltpu.CompilerParams(
            collective_id=0, has_side_effects=True, vmem_limit_bytes=56 * 2**20
        ),
    )(
        flat(fields), flat(cotangent), coarse_mask.transpose(2, 0, 1), *consts,
        *[held[name] for name in WEIGHTS],
    )
    shape = (LAT_ROWS, LON_COLS, LEVELS, FINE)
    return tuple(part.reshape(shape).transpose(2, 0, 1, 3) for part in (out, grad))


def solution(mesh):
    placed = (
        P(None, "lat", "lon", None),
        P("lon", None),
        P("lon", None),
        P("lon", None),
        P("lon", None),
        P("lon", None),
        P(None, "lat", "lon"),
        P(None, "lat", "lon", None),
    )

    def body(fields, w_fine_qkv, w_fine_out, w_merge, w_coarse_qkv, w_up, coarse_mask, cotangent):
        weights = (w_fine_qkv, w_fine_out, w_merge, w_up, w_coarse_qkv)
        return run_layer(mesh, fields, cotangent, coarse_mask, weights)

    return jax.shard_map(
        body,
        mesh=mesh,
        in_specs=placed,
        out_specs=(P(None, "lat", "lon", None), P(None, "lat", "lon", None)),
        check_vma=False,
    )
```

time: 759 us -> 125 us (0.16)
  waiting for transfers between devices: 427 us -> 0 us
  Pallas kernels: 0 us -> 122 us
  local copies, waits for them, and re-layouts: 82.3 us -> 2.37 us
  blocking collectives: 77.3 us -> 0 us
  starting transfers between devices: 71.1 us -> 0 us
  matrix products: 45 us -> 0 us
  other arithmetic: 35.6 us -> 0 us
  between operations: 15.5 us -> 0.65 us
    all_gather x5 -> x0, waiting for transfers between devices: 396 us -> none  [the longest x1 112 us: body(): lax.all_gather(local_pair, 'lon', axis=0, tiled=True)]
    pallas_call x0 -> x1, Pallas kernels: none -> 122 us  [run_layer(): pl.pallas_call(functools.partial(layer_kernel, mesh.shape['lon'], mesh.sh...]
    all_gather x1 -> x0, blocking collectives: 77.3 us -> none  [body(): lax.all_gather(w_fine_out, 'lon', axis=0, tiled=True)]
    ppermute x16 -> x0, starting transfers between devices: 70.9 us -> none  [the longest x8 50.4 us: passed_along(): lax.ppermute(shard, axis, [(i, (i + by) % size) for i in range(size)])]
    dot_general x24 -> x0, matrix products: 45 us -> none  [the longest x12 25.5 us: project(): product = jnp.dot(flat_rows, weight, preferred_element_type=jnp.float32)]
    ppermute x16 -> x0, waiting for transfers between devices: 28.7 us -> none  [the longest x8 25.7 us: passed_along(): lax.ppermute(shard, axis, [(i, (i + by) % size) for i in range(size)])]
    reshape x22 -> x0, local copies, waits for them, and re-layouts: 28.6 us -> none  [the longest x5 8.36 us: project(): flat_rows = values.reshape(-1, values.shape[-1])]
    reduce_sum x17 -> x0, other arithmetic: 14 us -> none  [the longest x2 3.87 us: attend(): row_peak = jnp.max(scores, axis=-1, keepdims=True)]
  transfers between devices with their start and end apart: 21 -> 0, of which waited for: 12 -> 0; matrix products, arithmetic and copies ran while one was open for 11% -> 0% of each run, Pallas kernels for 0% -> 0%
where the time goes in v1:
time: 125 us
  Pallas kernels  122 us (98%)
  local copies, waits for them, and re-layouts  2.37 us (2%)
    pallas_call x1, Pallas kernels, run_layer(): pl.pallas_call(functools.partial(layer_kernel, mesh.shape['lon'], mesh.sh...  122 us

profile of v1, /device:TPU:6, one launch (start us, length us, event | category | flops | bytes accessed | tf_op | source)
XLA Modules:
  0.0 125.0 jit_solution(9191356337165448649)
XLA Ops:
  0.6 122.0 %shard_map.176 = (bf16[72,2,512]{2,1,0:T(2,128)(2,1)}, bf16[72,2,512]{2,1,0:T(2,128)(2,1)}) custom-call(bf16[72,2,512]{2,1,0:T(2,128)(2,1)} %bitcast.13, bf16[72,2,512]{2,1,0:T(2,128)(2,1)} %bitcast.14, s32[3,2,6]{2,1,0:T(2,128)} %bitcast.17, f32[192,256]{1,0:T(8,128)} %constant.18.clone.refs_3_, f32[144,256]{1,0:T(8,128)} %constant.19.clone.refs_4_, ...), custom_call_target="tpu_custom_call" | custom-call | tf_op jit(solution)/shard_map/pallas_call | solution.py:802
  122.7 0.0 copy-start
  122.7 1.7 %copy.21 = bf16[2,12,6,512]{3,0,2,1:T(2,128)(2,1)} copy(bf16[2,12,6,512]{3,0,2,1:T(2,128)(2,1)} %bitcast.16) | data formatting | bytes 294912
  124.4 0.0 copy-done
  124.4 0.7 copy.22
Async XLA Ops:
  122.7 1.7 %copy-start = (bf16[72,2,512]{2,1,0:T(2,128)(2,1)S(1)}, bf16[72,2,512]{2,1,0:T(2,128)(2,1)}, u32[]{:S(2)}) copy-start(bf16[72,2,512]{2,1,0:T(2,128)(2,1)} %get-tuple-element.5) | copy-start | bytes 442372

commit v2 on v1

--- a/solution.py
+++ b/solution.py
@@ -156,8 +156,6 @@
     def one_group(group):
         stack_heads(stack, q[:, lanes(group)])
         scores[...] = mt(stack[...], kv[:, lanes(group)])
-        if pump is not None:
-            pump()
 
         def one_head(head, carry):
             spot = pl.ds(pl.multiple_of(head * together, 16), together)
@@ -166,9 +164,7 @@
             weights[group, spot, :] = short(e * (1.0 / jnp.sum(e, axis=-1, keepdims=True)))
             return carry
 
-        lax.fori_loop(0, HEADS * rows // together, one_head, 0, unroll=4 if together == rows else 1)
-        if pump is not None:
-            pump()
+        lax.fori_loop(0, HEADS * rows // together, one_head, 0, unroll=8 if together == rows else 1)
         out[:, lanes(group)] = join_heads(mm(weights[group], kv[:, lanes(group, channels)]), rows)
         if pump is not None:
             pump()
@@ -195,7 +191,7 @@
             inner[spot, :] = short(p * (d - mean) * (HD**-0.5))
             return carry
 
-        lax.fori_loop(0, HEADS * rows // together, one_head, 0, unroll=4 if together == rows else 1)
+        lax.fori_loop(0, HEADS * rows // together, one_head, 0, unroll=8 if together == rows else 1)
         dkv[:, lanes(group, channels)] = short(tm(weights[group], stack[...]))
         dq[:, lanes(group)] = join_heads(mm(inner[...], kv[:, lanes(group)]), rows)
         stack_heads(stack, q[:, lanes(group)])
@@ -266,7 +262,7 @@
     target[...] = short(jnp.stack(halves, axis=1))
 
 
-def layer(peers, send, steps, field, cot_field, mask_field, consts, out, grad_out, full, ready, s):
+def layer(peers, send, settle, steps, field, cot_field, mask_field, consts, out, grad_out, full, ready, s):
     pick, pick_t, shrink, spread, edge, rims, bands, own_bands, mask_place = consts
 
     def pump(count=1):
@@ -352,7 +348,6 @@
     blocks(KEYS // 128, norm_step)
     pump(2)
     project(s.fq, s.xn.at[pl.ds(0, OWN)], FQ)
-    pump()
     project(s.fkv, s.xn, FQ, FINE)
     pump()
     attend(OWN, FINE, s.fq, s.fkv, s.fbias, s.mixed, s.fstack, s.fscores, s.fweights, pump)
@@ -419,6 +414,7 @@
         s.d_normed[:, at] = s.d_normed[:, at] + own_part
 
     blocks(COARSE // GROUP, own_step)
+    settle(len(back_copies))
     for copy in back_copies:
         copy.wait_recv()
     d_normed = s.d_normed[...]
@@ -466,6 +462,7 @@
         s.d_fine[:, at] = s.d_fine[:, at] + own_part
 
     blocks(FINE // GROUP, query_step)
+    settle(len(end_copies))
     for copy in end_copies:
         copy.wait_recv()
     d_fine = s.d_fine[...] + wide(s.mate_got[...])
@@ -637,7 +634,7 @@
         shift.start()
 
     fine = (FQ, FO)
-    fine_z = [send(own[k], here(k), peer) for peer in (up_z, down_z) + peers[9:] for k in fine]
+    fine_z = [[send(own[k], here(k), peer) for peer in (up_z, down_z) + peers[9:]] for k in fine]
     ring[MG] = [send(own[MG], here(MG), peer) for peer in (up_z, down_z)]
 
     @pl.when(x == 0)
@@ -651,60 +648,64 @@
     ring[CQ] = [pass_on(CQ, (z, w, c), peer) for peer in (up_z, down_z)]
     chain_across(CQ, 0)
     yield
-    arrived(fine_z)
-    fine_y = []
-    for k in fine:
+    fine_y, fine_far = {}, {}
+
+    def fine_round(k):
+        arrived(fine_z[k])
         locals_[k].wait()
-        fine_y += across_y(k, every)
-    for k in fine:
+        fine_y[k] = across_y(k, every)
         to_twin(k, (every, y, c))
-    across[MG, 0] = [send(own[MG], here(MG), peer) for peer in (up_y, down_y)]
-    yz_start(UP)
-    yield
-    chain_step(CQ, 1)
-    chain_step(MG, 1)
-    yield
-    chain_step(CQ, 2)
-    chain_step(MG, 2)
-    yield
-    arrived(fine_y)
-    fine_far = []
-    for k in fine:
-        fine_far += [
+
+    def fine_spread(k):
+        arrived(fine_y[k])
+        fine_far[k] = [
             pass_on(k, (pl.ds(0, 4), y_at(-1), c), up_y),
             pass_on(k, (pl.ds(4, 4), y_at(1), c), down_y),
         ]
-    for k in fine:
         to_twin(k, (every, y_at(-1), c))
         to_twin(k, (every, y_at(1), c))
+
+    fine_round(FQ)
+    fine_round(FO)
+    across[MG, 0] = [send(own[MG], here(MG), peer) for peer in (up_y, down_y)]
+    yz_start(UP)
+    yield
+    chain_step(CQ, 1)
+    chain_step(MG, 1)
+    yield
+    fine_spread(FQ)
+    chain_step(CQ, 2)
+    chain_step(MG, 2)
+    yield
+    fine_spread(FO)
     chain_step(CQ, 3)
     chain_step(MG, 3)
-    yz_far(UP)
-    yield
-    arrived(fine_far)
-    for k in fine:
-        to_twin(k, (every, y_at(2), c))
+    yield
+    arrived(fine_far[FQ])
+    to_twin(FQ, (every, y_at(2), c))
     chain_step(CQ, 4)
     chain_step(MG, 4)
+    arrived(fine_far[FO])
+    to_twin(FO, (every, y_at(2), c))
+    arrived(twins[FQ])
+
+    def tidy(part):
+        columns = wide_columns(part, 0, FINE)
+        s.w_fq[:, columns] = short(wide(full[FQ][:, :, :, :, columns]).reshape(FINE, FINE))
+
+    blocks(3, tidy)
+    ready.add(FQ)
+    yield
     locals_[MG].wait()
-    yield
     chain_spread(CQ, 0, 0)
     chain_spread(MG, 0, 0)
     chain_twins(CQ, (0,))
     chain_twins(MG, (0,))
-    yz_round(UP)
-    yield
-    arrived(twins[FQ])
-
-    def tidy(part):
-        columns = wide_columns(part, 0, FINE)
-        s.w_fq[:, columns] = short(wide(full[FQ][:, :, :, :, columns]).reshape(FINE, FINE))
-
-    blocks(3, tidy)
-    ready.add(FQ)
+    yz_far(UP)
     chain_spread(CQ, 7, 1)
     chain_spread(MG, 7, 1)
     yield
+    yz_round(UP)
     arrived(twins[FO])
     s.w_fo[...] = short(wide(full[FO][...]).reshape(FINE, FINE))
     ready.add(FO)
@@ -783,14 +784,21 @@
         started.append(None if wait_start else copy)
         return copy
 
+    settled = [0]
+
+    def settle(but):
+        upto = len(started) - but
+        for copy in started[settled[0] : upto]:
+            if copy is not None:
+                copy.wait_send()
+        settled[0] = upto
+
     ready = set()
     steps = gather_steps(spot, rings, own, full, send, local_sems, ready, scratch)
     layer(
-        peers, send, steps, field, cot_field, mask_field, consts, out, grad_out, full, ready, scratch
+        peers, send, settle, steps, field, cot_field, mask_field, consts, out, grad_out, full, ready, scratch
     )
-    for copy in started:
-        if copy is not None:
-            copy.wait_send()
+    settle(0)
 
 
 def run_layer(mesh, fields, cotangent, coarse_mask, held):

time: 125 us -> 124 us (level)
  no operation moved by 1% of the time
where the time goes in v2:
time: 124 us
  Pallas kernels  121 us (98%)
  local copies, waits for them, and re-layouts  2.37 us (2%)
    pallas_call x1, Pallas kernels, run_layer(): pl.pallas_call(functools.partial(layer_kernel, mesh.shape['lon'], mesh.sh...  121 us

profile of v2, /device:TPU:6, one launch (start us, length us, event | category | flops | bytes accessed | tf_op | source)
XLA Modules:
  0.0 123.9 jit_solution(14936411329862093105)
XLA Ops:
  0.6 120.9 %shard_map.176 = (bf16[72,2,512]{2,1,0:T(2,128)(2,1)}, bf16[72,2,512]{2,1,0:T(2,128)(2,1)}) custom-call(bf16[72,2,512]{2,1,0:T(2,128)(2,1)} %bitcast.13, bf16[72,2,512]{2,1,0:T(2,128)(2,1)} %bitcast.14, s32[3,2,6]{2,1,0:T(2,128)} %bitcast.17, f32[192,256]{1,0:T(8,128)} %constant.18.clone.refs_3_, f32[144,256]{1,0:T(8,128)} %constant.19.clone.refs_4_, ...), custom_call_target="tpu_custom_call" | custom-call | tf_op jit(solution)/shard_map/pallas_call | solution.py:810
  121.5 0.0 copy-start
  121.6 1.7 %copy.21 = bf16[2,12,6,512]{3,0,2,1:T(2,128)(2,1)} copy(bf16[2,12,6,512]{3,0,2,1:T(2,128)(2,1)} %bitcast.16) | data formatting | bytes 294912
  123.3 0.0 copy-done
  123.3 0.7 copy.22
Async XLA Ops:
  121.5 1.7 %copy-start = (bf16[72,2,512]{2,1,0:T(2,128)(2,1)S(1)}, bf16[72,2,512]{2,1,0:T(2,128)(2,1)}, u32[]{:S(2)}) copy-start(bf16[72,2,512]{2,1,0:T(2,128)(2,1)} %get-tuple-element.5) | copy-start | bytes 442372
